TPU v7x, 32 devices: a whole 2x2x4 slice. The times are simulated.
32 devices in a mesh: parts: 2 (over y), dp: 4 (over z), tensor: 4 (over x, core).
Axes of the slice: x: 2, y: 2, z: 4, core: 2. Of those that a mesh axis runs over, the one named last changes fastest.
Arguments:
- tokens: bfloat16 [4096, 8192], P(('parts', 'dp'), 'tensor'), parts along dimension 0, may hold values from -6 to 6
- value_weight: bfloat16 [8192, 1024], P('tensor'), may hold values from -0.0625 to 0.0625
- down_panels: bfloat16 [12, 64, 8192], P('dp', None, 'tensor'), may hold values from -0.0625 to 0.0625
- up_panels: bfloat16 [12, 64, 1024], P('dp', None, 'tensor'), may hold values from -0.75 to 0.75
- adapter_rank: int32 [12], replicated, may hold values from 1 to 4
- adapter_slot: int32 [24], P('parts'), parts along dimension 0, may hold values from 0 to 11, as said below
- seg_adapter: int32 [8, 32], P(('parts', 'dp')), parts along dimension 0, may hold values from 0 to 11, as said below
- seg_lengths: int32 [8, 32], P(('parts', 'dp')), parts along dimension 0, may hold values from 1 to 64, 512 in all within a row
Outputs:
- projected: bfloat16 [4096, 1024], P(('parts', 'dp'), 'tensor'), parts along dimension 0
There are 2 independent parts, one for each index of `parts`. A program takes and returns all parts, laid end to end along the dimension named above; an argument that names none is the same for every part. Nothing has to cross between parts.
Inputs may be any that keep to these rules, and one draw needn't show every extreme that they name: A permutation: adapter a is stored in row adapter_slot[a] of the panels, that is on dp index adapter_slot[a] // 3. `seg_adapter`: the requests of one replica name adapters stored on any one dp index at most 16 times, and exactly 16 times for some dp index in every replica. `seg_lengths`: each row sums to 512.
All inputs are finite; a program needn't handle non-finite values.
Results may differ from a plain program's by a relative error of at most 0.013.
Values may be sent and summed in bfloat16 or wider, within the bound.
A program may use at most 128 MiB of HBM per device.

v0:
```python
import jax
import jax.numpy as jnp
from jax import lax
from jax.sharding import PartitionSpec as P

LONGEST_TOKENS = 64


def local(
    tokens,
    value_weight,
    down_panels,
    up_panels,
    adapter_rank,
    adapter_slot,
    seg_adapter,
    seg_lengths,
):
    token_count = tokens.shape[0]
    rank_pad = down_panels.shape[1]
    feature_share = up_panels.shape[2]
    lengths = seg_lengths[0]
    named = seg_adapter[0]
    requests_here = lengths.shape[0]
    partial_values = jnp.dot(tokens, value_weight, preferred_element_type=jnp.float32)
    base_output = lax.psum_scatter(
        partial_values.astype(jnp.bfloat16), "tensor", scatter_dimension=1, tiled=True
    ).astype(jnp.float32)
    seg_starts = jnp.cumsum(lengths) - lengths
    window_start = jnp.minimum(seg_starts, token_count - LONGEST_TOKENS)
    storage_row = adapter_slot[named]
    ranks = adapter_rank[storage_row] * 16
    empty_down = jnp.zeros((requests_here, rank_pad, down_panels.shape[2]), jnp.bfloat16)
    empty_up = jnp.zeros((requests_here, rank_pad, feature_share), jnp.bfloat16)
    pieces = (
        lax.all_gather(down_panels, "dp", axis=0, tiled=True),
        lax.all_gather(up_panels, "dp", axis=0, tiled=True),
    )
    count_rows = pieces[0].shape[0]
    inside = (storage_row >= 0) & (storage_row < count_rows)
    picked = jnp.clip(storage_row, 0, count_rows - 1)
    new_down = jnp.where(inside[:, None, None], pieces[0][picked], empty_down)
    new_up = jnp.where(inside[:, None, None], pieces[1][picked], empty_up)
    window_rows = window_start[:, None] + jnp.arange(LONGEST_TOKENS, dtype=jnp.int32)[None, :]
    gathered = tokens[window_rows]
    shrink = jnp.einsum("smd,srd->smr", gathered, new_down, preferred_element_type=jnp.float32)
    inside_rows = (window_rows >= seg_starts[:, None]) & (
        window_rows < (seg_starts + lengths)[:, None]
    )
    keep_cols = jnp.arange(rank_pad, dtype=jnp.int32)[None, :] < ranks[:, None]
    shrink = jnp.where(inside_rows[:, :, None] & keep_cols[:, None, :], shrink, 0.0)
    summed = lax.psum(
        shrink.reshape(requests_here, LONGEST_TOKENS * rank_pad).astype(jnp.bfloat16), "tensor"
    ).astype(jnp.float32)
    narrow = summed.reshape(requests_here, LONGEST_TOKENS, rank_pad).astype(jnp.bfloat16)
    adapter_update = jnp.einsum("smr,srk->smk", narrow, new_up, preferred_element_type=jnp.float32)
    adapter_update = adapter_update * (32.0 / ranks.astype(jnp.float32))[:, None, None]
    adapter_output = (
        jnp.zeros((token_count, feature_share), jnp.float32)
        .at[window_rows.reshape(-1)]
        .add(adapter_update.reshape(-1, feature_share))
    )
    return (base_output + adapter_output).astype(jnp.bfloat16)


def solution(mesh):
    return jax.shard_map(
        local,
        mesh=mesh,
        in_specs=(
            P(("parts", "dp"), "tensor"),
            P("tensor", None),
            P("dp", None, "tensor"),
            P("dp", None, "tensor"),
            P(),
            P("parts"),
            P(("parts", "dp"), None),
            P(("parts", "dp"), None),
        ),
        out_specs=P(("parts", "dp"), "tensor"),
        check_vma=False,
    )
```

profile of v0, /device:TPU:0, one launch (start us, length us, event | category | flops | bytes accessed | tf_op | source)
XLA Modules:
  0.0 152.6 jit_solution(7159469861857903883)
XLA Ops:
  7.4 0.0 copy-start
  7.4 0.0 all-gather.2.cloned.1.call-start
  7.4 0.7 all-gather.2.cloned.1.call-update
  8.1 0.0 copy-start.5
  8.1 0.0 copy-start.1
  8.1 0.0 copy-start.4
  8.1 0.0 copy-start.3
  8.1 0.0 reduce-scatter.2.cloned.1.call-start
  8.2 0.8 copy-done
  9.0 5.5 %convolution_convert_fusion = bf16[512,1024]{1,0:T(8,128)(2,1)} fusion(bf16[512,2048]{1,0:T(8,128)(2,1)S(1)} %copy-done, bf16[2048,1024]{1,0:T(8,128)(2,1)} %param.9), kind=kOutput, calls=%fused_computation.11 | convolution fusion | flops 2148007936 | bytes 7340032 | tf_op jit(solution)/shard_map/dot_general | solution.py:25
  14.5 0.0 reduce-scatter.2.cloned.1.call-update
  14.5 0.0 all-reduce.2.cloned.1.call-start
  14.5 0.0 copy-done.5
  14.6 0.0 copy-done.1
  14.6 0.7 gather_fusion
  15.3 0.0 copy-done.4
  15.3 0.1 copy.11
  15.4 0.1 reduce-window.7
  15.4 0.1 reduce
  15.6 0.1 compare_select_fusion.1
  15.6 0.1 iota_add_fusion
  15.7 0.1 reshape.269
  15.8 0.1 add.111
  15.9 0.0 copy-done.3
  15.9 21.3 %all_gather.7 = bf16[12,64,256]{2,1,0:T(8,128)(2,1)S(1)} all-gather(bf16[3,64,256]{2,1,0:T(8,128)(2,1)S(1)} %copy-done.3), channel_id=1, replica_groups=mesh['parts'=2,'dp'=4,'tensor'=4] {'dp'}, dimensions={0}, use_global_device_ids=true | all-gather | bytes 491520 | tf_op jit(solution)/shard_map/all_gather | solution.py:37
  37.2 0.0 copy-start.2
  37.2 11.0 %gather_fusion.2 = bf16[2048,2048]{1,0:T(8,128)(2,1)} fusion(bf16[512,2048]{1,0:T(8,128)(2,1)S(1)} %copy-done, s32[2048]{0:T(1024)S(1)} %broadcast_clamp_fusion), kind=kCustom, calls=%fused_computation.2 | custom fusion | bytes 16785408 | tf_op jit(solution)/shard_map/gather | solution.py:45
  48.1 0.0 copy-done.2
  48.1 0.7 gather_fusion.1
  48.8 1.6 %gather_fusion.4 = bf16[32,64,256]{2,1,0:T(8,128)(2,1)} fusion(bf16[12,64,256]{2,1,0:T(8,128)(2,1)S(1)} %all_gather.7, s32[1024]{0:T(1024)S(1)} %pad_clamp_fusion), kind=kCustom, calls=%fused_computation.4 | custom fusion | bytes 2097280 | tf_op jit(solution)/shard_map/gather | solution.py:43
  50.5 0.1 iota_compare_fusion
  50.6 29.6 %all-gather.2.cloned.1.call-done = bf16[12,64,2048]{2,1,0:T(8,128)(2,1)} async-done(((bf16[3,64,2048]{2,1,0:T(8,128)(2,1)}), bf16[12,64,2048]{2,1,0:T(8,128)(2,1)}) %all-gather.2.cloned.1.call-update) | async-done | bytes 3145744 | tf_op jit(solution)/shard_map/all_gather | solution.py:36
  80.2 6.9 %gather_fusion.3 = bf16[32,64,2048]{2,1,0:T(8,128)(2,1)} fusion(bf16[12,64,2048]{2,1,0:T(8,128)(2,1)} %all-gather.2.cloned.1.call-done, s32[1024]{0:T(1024)S(1)} %pad_clamp_fusion), kind=kCustom, calls=%fused_computation.3 | custom fusion | bytes 16777344 | tf_op jit(solution)/shard_map/gather | solution.py:42
  87.0 9.0 %fusion.7 = bf16[32,64,64]{2,1,0:T(8,128)(2,1)} fusion(bf16[32,64,2048]{2,1,0:T(8,128)(2,1)} %bitcast.26, bf16[32,64,2048]{2,1,0:T(8,128)(2,1)} %gather_fusion.3, pred[32]{0:T(512)(128)(4,1)S(1)} %compare_and_fusion.1, pred[32,64]{1,0:T(8,128)(4,1)S(1)} %get-tuple-element.9, pred[32,64]{1,0:T(8,128)(4,1)S(1)} %get-tuple-element.10), kind=kOutput, calls=%fused_computation.13 | convolution fusion | flops 541458432 | bytes 17043488 | tf_op jit(solution)/shard_map/smd,srd->smr/dot_general | solution.py:46
  96.0 0.0 all-reduce.2.cloned.1.call-update
  96.1 0.0 reduce-scatter.2.cloned.1.call-done
  96.1 1.0 convert_element_type.28
  97.1 32.0 %all-reduce.2.cloned.1.call-done = bf16[32,64,64]{2,1,0:T(8,128)(2,1)} async-done(((bf16[32,64,64]{2,1,0:T(8,128)(2,1)}), bf16[32,64,64]{2,1,0:T(8,128)(2,1)}) %all-reduce.2.cloned.1.call-update) | async-done | bytes 262160 | tf_op jit(solution)/shard_map/psum | solution.py:52
  129.1 3.2 %convolution_multiply_fusion = f32[32,64,256]{2,1,0:T(8,128)} fusion(bf16[32,64,64]{2,1,0:T(8,128)(2,1)} %all-reduce.2.cloned.1.call-done, f32[32]{0:T(128)S(1)} %convert_divide_fusion, bf16[32,64,256]{2,1,0:T(8,128)(2,1)} %gather_fusion.4, pred[32]{0:T(512)(128)(4,1)S(1)} %compare_and_fusion.1), kind=kOutput, calls=%fused_computation.10 | convolution fusion | flops 68157440 | bytes 3408032 | tf_op jit(solution)/shard_map/smr,srk->smk/dot_general | solution.py:56
  132.3 12.2 %scatter_fusion = f32[512,256]{1,0:T(8,128)S(1)} fusion(f32[512,256]{1,0:T(8,128)S(1)} %convert_element_type.28, s32[2048]{0:T(1024)S(1)} %bitcast.28, f32[2048,256]{1,0:T(8,128)} %bitcast.27), kind=kCustom, calls=%fused_computation.5 | custom fusion | flops 524288 | bytes 6299648 | tf_op jit(solution)/shard_map/scatter-add | solution.py:61
  144.5 0.7 convert_element_type.33
  (11 shorter events, 0.1 us)
Async XLA Ops:
  7.4 1.6 %copy-start = (bf16[512,2048]{1,0:T(8,128)(2,1)S(1)}, bf16[512,2048]{1,0:T(8,128)(2,1)}, u32[]{:S(2)}) copy-start(bf16[512,2048]{1,0:T(8,128)(2,1)} %param.8) | copy-start | bytes 6291460
  7.4 72.8 %all-gather.2.cloned.1.call-start = ((), (), s32[]{:S(2)}) async-start(), calls=%async_computation.2 | async-start | bytes 3932160 | tf_op jit(solution)/shard_map/all_gather | solution.py:36
  8.1 6.4 %copy-start.5 = (s32[1,32]{1,0:T(1,128)S(1)}, s32[1,32]{1,0:T(1,128)}, u32[]{:S(2)}) copy-start(s32[1,32]{1,0:T(1,128)} %param.14) | copy-start | bytes 388
  8.1 6.5 %copy-start.1 = (s32[12]{0:T(128)S(1)}, s32[12]{0:T(128)}, u32[]{:S(2)}) copy-start(s32[12]{0:T(128)} %param.13) | copy-start | bytes 148
  8.1 7.2 %copy-start.4 = (s32[1,32]{1,0:T(1,128)S(1)}, s32[1,32]{1,0:T(1,128)}, u32[]{:S(2)}) copy-start(s32[1,32]{1,0:T(1,128)} %param.15) | copy-start | bytes 388
  8.1 7.8 %copy-start.3 = (bf16[3,64,256]{2,1,0:T(8,128)(2,1)S(1)}, bf16[3,64,256]{2,1,0:T(8,128)(2,1)}, u32[]{:S(2)}) copy-start(bf16[3,64,256]{2,1,0:T(8,128)(2,1)} %param.11) | copy-start | bytes 294916
  8.1 88.0 %reduce-scatter.2.cloned.1.call-start = ((), (), s32[]{:S(2)}) async-start(), calls=%async_computation.1 | async-start | bytes 1310720 | tf_op jit(solution)/shard_map/reduce_scatter | solution.py:26
  14.5 114.6 %all-reduce.2.cloned.1.call-start = ((), (), s32[]{:S(2)}) async-start(), calls=%async_computation.3 | async-start | bytes 1048576 | tf_op jit(solution)/shard_map/psum | solution.py:52
  37.2 11.0 %copy-start.2 = (s32[12]{0:T(128)S(1)}, s32[12]{0:T(128)}, u32[]{:S(2)}) copy-start(s32[12]{0:T(128)} %param.12) | copy-start | bytes 148
Sparse Core Ops, SparseCore 0:
  9.8 70.3 all-gather.1
Sparse Core Ops, SparseCore 1:
  14.6 27.5 reduce-scatter.1
  96.1 32.9 all-reduce.1
where the time goes:
time: 153 us
  waiting for transfers between devices  62.4 us (41%)
  local copies, waits for them, and re-layouts  21.8 us (14%)
  blocking collectives  21.3 us (14%)
  matrix products  17.7 us (12%)
  between operations  15 us (10%)
  other arithmetic  14.4 us (9%)
    psum x1, waiting for transfers between devices, local(): lax.psum(shrink.reshape(requests_here, LONGEST_TOKENS * rank_pad).astype(...  32 us
    all_gather x1, waiting for transfers between devices, local(): lax.all_gather(down_panels, 'dp', axis=0, tiled=True)  29.6 us
    all_gather x1, blocking collectives, local(): lax.all_gather(up_panels, 'dp', axis=0, tiled=True)  21.3 us
    scatter-add x1, other arithmetic, local(): adapter_output = jnp.zeros((token_count, feature_share), jnp.float32).at[...  12.2 us
    gather x1, local copies, waits for them, and re-layouts, local(): gathered = tokens[window_rows]  11 us
    dot_general x1, matrix products, local(): jnp.einsum('smd,srd->smr', gathered, new_down, preferred_element_type=jnp...  8.98 us
    gather x1, local copies, waits for them, and re-layouts, local(): new_down = jnp.where(inside[:, None, None], pieces[0][picked], empty_down)  6.85 us
    dot_general x1, matrix products, local(): jnp.dot(tokens, value_weight, preferred_element_type=jnp.float32)  5.49 us
  transfers between devices with their start and end apart: 3, of which 2 were waited for; matrix products, arithmetic and copies ran while one was open for 24% of the time, Pallas kernels for 0%

commit v1 on v0

v1 whole, which is shorter than its diff:
```python
import jax
import jax.numpy as jnp
from jax import lax
from jax.sharding import PartitionSpec as P


def local(
    tokens,
    value_weight,
    down_panels,
    up_panels,
    adapter_rank,
    adapter_slot,
    seg_adapter,
    seg_lengths,
):
    token_count, share = tokens.shape
    rank_pad = down_panels.shape[1]
    feature_share = up_panels.shape[2]
    adapters = adapter_rank.shape[0]
    lengths = seg_lengths[0]
    named = seg_adapter[0]
    down_all = lax.all_gather(down_panels, "dp", axis=0, tiled=True)
    up_all = lax.all_gather(up_panels, "dp", axis=0, tiled=True)
    partial_values = jnp.dot(tokens, value_weight, preferred_element_type=jnp.float32)
    base_output = lax.psum_scatter(
        partial_values.astype(jnp.bfloat16), "tensor", scatter_dimension=1, tiled=True
    ).astype(jnp.float32)
    ends = jnp.cumsum(lengths)
    position = jnp.arange(token_count, dtype=jnp.int32)[:, None]
    in_request = (position >= (ends - lengths)[None, :]) & (position < ends[None, :])
    storage_row = adapter_slot[named]
    token_row = jnp.sum(jnp.where(in_request, storage_row[None, :], 0), axis=1)
    column = jnp.arange(adapters * rank_pad, dtype=jnp.int32)
    column_row = column // rank_pad
    column_keep = column % rank_pad < 16 * adapter_rank[column_row]
    mask = (token_row[:, None] == column_row[None, :]) & column_keep[None, :]
    wide = lax.dot_general(
        tokens,
        down_all.reshape(adapters * rank_pad, share),
        (((1,), (1,)), ((), ())),
        preferred_element_type=jnp.float32,
    )
    shrink = jnp.where(mask, wide, 0.0).reshape(token_count, adapters, rank_pad).sum(axis=1)
    summed = lax.psum(shrink.astype(jnp.bfloat16), "tensor")
    spread = jnp.where(mask, jnp.tile(summed, (1, adapters)), 0)
    update = jnp.dot(
        spread, up_all.reshape(adapters * rank_pad, feature_share), preferred_element_type=jnp.float32
    )
    token_rank = (16 * adapter_rank[token_row]).astype(jnp.float32)
    return (base_output + update * (32.0 / token_rank)[:, None]).astype(jnp.bfloat16)


def solution(mesh):
    return jax.shard_map(
        local,
        mesh=mesh,
        in_specs=(
            P(("parts", "dp"), "tensor"),
            P("tensor", None),
            P("dp", None, "tensor"),
            P("dp", None, "tensor"),
            P(),
            P("parts"),
            P(("parts", "dp"), None),
            P(("parts", "dp"), None),
        ),
        out_specs=P(("parts", "dp"), "tensor"),
        check_vma=False,
    )
```

time: 153 us -> 132 us (0.86)
  local copies, waits for them, and re-layouts: 21.8 us -> 5.36 us
  matrix products: 17.7 us -> 12.8 us
  other arithmetic: 14.4 us -> 17.4 us
  waiting for transfers between devices: 62.4 us -> 59.9 us
    gather x4 -> x1, local copies, waits for them, and re-layouts: 20.1 us -> 0.68 us  [local(): column_keep = column % rank_pad < 16 * adapter_rank[column_row]]
    scatter-add x1 -> x0, other arithmetic: 12.2 us -> none  [local(): adapter_output = jnp.zeros((token_count, feature_share), jnp.float32).at[...]
    gather x3 -> x8, other arithmetic: 0.02 us -> 8.79 us  [the longest x6 4.46 us: local(): column_keep = column % rank_pad < 16 * adapter_rank[column_row]]
    dot_general x2, matrix products: 12.2 us -> 7.28 us  [the longest x1 4.89 us: local(): lax.dot_general(tokens, down_all.reshape(adapters * rank_pad, share), (((...]
    div x1, other arithmetic: 0.01 us -> 3.08 us  [local(): 32.0 / token_rank]
    lt x1 -> x2, other arithmetic: 0.08 us -> 3.1 us  [local(): column_keep = column % rank_pad < 16 * adapter_rank[column_row]]
    select_n x1, local copies, waits for them, and re-layouts: 0.07 us -> 3.03 us  [local(): jnp.where(mask, wide, 0.0).reshape(token_count, adapters, rank_pad)]
    psum x1, waiting for transfers between devices: 32 us -> 29.7 us  [local(): summed = lax.psum(shrink.astype(jnp.bfloat16), 'tensor')]
  transfers between devices with their start and end apart: 3 -> 3, of which waited for: 2 -> 2; matrix products, arithmetic and copies ran while one was open for 24% -> 25% of each run, Pallas kernels for 0% -> 0%
where the time goes in v1:
time: 132 us
  waiting for transfers between devices  59.9 us (45%)
  blocking collectives  21.3 us (16%)
  other arithmetic  17.4 us (13%)
  between operations  15 us (11%)
  matrix products  12.8 us (10%)
  local copies, waits for them, and re-layouts  5.36 us (4%)
    psum x1, waiting for transfers between devices, local(): summed = lax.psum(shrink.astype(jnp.bfloat16), 'tensor')  29.7 us
    all_gather x1, waiting for transfers between devices, local(): down_all = lax.all_gather(down_panels, 'dp', axis=0, tiled=True)  29.5 us
    all_gather x1, blocking collectives, local(): up_all = lax.all_gather(up_panels, 'dp', axis=0, tiled=True)  21.3 us
    dot_general x1, matrix products, local(): jnp.dot(tokens, value_weight, preferred_element_type=jnp.float32)  5.54 us
    dot_general x1, matrix products, local(): lax.dot_general(tokens, down_all.reshape(adapters * rank_pad, share), (((...  4.89 us
    gather x6, other arithmetic, local(): column_keep = column % rank_pad < 16 * adapter_rank[column_row]  4.46 us
    gather x2, other arithmetic, local(): token_rank = (16 * adapter_rank[token_row]).astype(jnp.float32)  4.33 us
    lt x2, other arithmetic, local(): column_keep = column % rank_pad < 16 * adapter_rank[column_row]  3.1 us
  transfers between devices with their start and end apart: 3, of which 2 were waited for; matrix products, arithmetic and copies ran while one was open for 25% of the time, Pallas kernels for 0%

profile of v1, /device:TPU:0, one launch (start us, length us, event | category | flops | bytes accessed | tf_op | source)
XLA Modules:
  0.0 131.9 jit_solution(10149404406821536575)
XLA Ops:
  7.4 0.0 copy-start
  7.4 0.0 all-gather.2.cloned.1.call-start
  7.4 0.7 all-gather.2.cloned.1.call-update
  8.1 0.0 copy-start.3
  8.1 0.0 copy-start.5
  8.1 0.0 copy-start.4
  8.1 0.0 copy-start.1
  8.1 0.0 copy-start.2
  8.1 0.0 reduce-scatter.2.cloned.1.call-start
  8.2 0.8 copy-done
  9.0 5.5 %convolution_convert_fusion = bf16[512,1024]{1,0:T(8,128)(2,1)} fusion(bf16[512,2048]{1,0:T(8,128)(2,1)S(1)} %copy-done, bf16[2048,1024]{1,0:T(8,128)(2,1)} %param.9), kind=kOutput, calls=%fused_computation.3 | convolution fusion | flops 2148007936 | bytes 7340032 | tf_op jit(solution)/shard_map/dot_general | solution.py:25
  14.5 0.0 reduce-scatter.2.cloned.1.call-update
  14.5 0.0 all-reduce.2.cloned.1.call-start
  14.7 0.0 copy-done.3
  14.7 0.7 fusion.29
  15.4 4.3 %fusion.23 = s32[768]{0:T(1024)S(1)} fusion(s32[]{:T(128)} %bitcast.9, s32[]{:T(128)} %bitcast.10, s32[]{:T(128)} %bitcast.11, s32[]{:T(128)} %bitcast.12, s32[]{:T(128)} %bitcast.13, s32[]{:T(128)} %bitcast.15, s32[]{:T(128)} %bitcast.14), kind=kLoop, calls=%fused_computation.69 | loop fusion | flops 17664 | bytes 3100 | tf_op jit(solution)/shard_map/gather | solution.py:36
  19.7 3.1 %fusion.21 = (pred[768]{0:T(1024)(128)(4,1)S(1)}, s32[768]{0:T(1024)S(1)}) fusion(pred[768]{0:T(1024)(128)(4,1)S(1)} %compare_reduce_fusion, pred[768]{0:T(1024)(128)(4,1)S(1)} %compare_reduce_fusion.1, pred[768]{0:T(1024)(128)(4,1)S(1)} %compare_reduce_fusion.2, pred[768]{0:T(1024)(128)(4,1)S(1)} %compare_reduce_fusion.3, ...), kind=kLoop, calls=%fused_computation.65 | loop fusion | flops 9984 | bytes 10772 | tf_op jit(solution)/shard_map/lt | solution.py:36
  22.8 0.0 copy-done.5
  22.8 0.0 copy-done.4
  22.9 0.1 copy.14
  22.9 0.1 reduce-window.4
  23.0 0.1 reduce
  23.1 0.1 mul.34
  23.2 0.0 copy-done.1
  23.2 0.7 gather_fusion
  23.9 0.1 select_reduce_fusion
  24.0 4.3 %compare_select_fusion.8 = (s32[512,1]{0,1:T(1,128)S(1)}, s32[512,1]{0,1:T(1,128)S(1)}) fusion(s32[]{:T(128)} %bitcast.9, s32[]{:T(128)} %bitcast.10, s32[]{:T(128)} %bitcast.11, s32[]{:T(128)} %bitcast.12, s32[]{:T(128)} %bitcast.13, s32[]{:T(128)} %bitcast.15, s32[]{:T(128)} %bitcast.14, s32[512,1]{0,1:T(1,128)S(1)} %bitcast.41), kind=kLoop, calls=%fused_computation.53 | loop fusion | flops 7680 | bytes 6172 | tf_op jit(solution)/shard_map/gather | solution.py:50
  28.3 0.0 copy-done.2
  28.3 21.3 %all_gather.7 = bf16[12,64,256]{2,1,0:T(8,128)(2,1)S(1)} all-gather(bf16[3,64,256]{2,1,0:T(8,128)(2,1)S(1)} %copy-done.2), channel_id=1, replica_groups=mesh['parts'=2,'dp'=4,'tensor'=4] {'dp'}, dimensions={0}, use_global_device_ids=true | all-gather | bytes 491520 | tf_op jit(solution)/shard_map/all_gather | solution.py:24
  49.7 3.1 %fusion.25 = f32[512]{0:T(512)S(1)} fusion(pred[512]{0:T(512)(128)(4,1)S(1)} %get-tuple-element.9, pred[512]{0:T(512)(128)(4,1)S(1)} %get-tuple-element.8, pred[512]{0:T(512)(128)(4,1)S(1)} %get-tuple-element.7, pred[512]{0:T(512)(128)(4,1)S(1)} %get-tuple-element.6, pred[512]{0:T(512)(128)(4,1)S(1)} %get-tuple-element.5, s32[512]{0:T(512)S(1)} %bitcast.42, ...), kind=kLoop, calls=%fused_computation.73 | loop fusion | flops 4096 | bytes 6676 | tf_op jit(solution)/shard_map/div | solution.py:51
  52.8 29.5 %all-gather.2.cloned.1.call-done = bf16[12,64,2048]{2,1,0:T(8,128)(2,1)} async-done(((bf16[3,64,2048]{2,1,0:T(8,128)(2,1)}), bf16[12,64,2048]{2,1,0:T(8,128)(2,1)}) %all-gather.2.cloned.1.call-update) | async-done | bytes 3145744 | tf_op jit(solution)/shard_map/all_gather | solution.py:23
  82.3 4.9 %and_select_fusion = f32[512,768]{1,0:T(8,128)} fusion(bf16[512,2048]{1,0:T(8,128)(2,1)S(1)} %copy-done, bf16[768,2048]{1,0:T(8,128)(2,1)} %bitcast.44, s32[768]{0:T(1024)S(1)} %add_select_fusion.2, s32[512]{0:T(512)S(1)} %select_reduce_fusion, pred[768]{0:T(1024)(128)(4,1)S(1)} %get-tuple-element.12), kind=kOutput, calls=%fused_computation.1 | convolution fusion | flops 1611792384 | bytes 6821632 | tf_op jit(solution)/shard_map/dot_general | solution.py:38
  87.2 3.0 %copy.15 = f32[512,768]{0,1:T(8,128)} copy(f32[512,768]{1,0:T(8,128)} %and_select_fusion) | data formatting | bytes 3145728 | tf_op jit(solution)/shard_map/jit(_where)/select_n | solution.py:44
  90.2 2.2 %reduce_sum.21 = bf16[512,64]{0,1:T(8,128)(2,1)} reduce(f32[512,12,64]{0,2,1:T(8,128)} %bitcast.40, f32[]{:T(128)} %constant.54.clone.1), dimensions={1}, to_apply=%region_3.4 | reduce | flops 360448 | bytes 1638404 | tf_op jit(solution)/shard_map/reduce_sum | solution.py:44
  92.4 0.0 all-reduce.2.cloned.1.call-update
  92.4 0.0 reduce-scatter.2.cloned.1.call-done
  92.4 29.7 %all-reduce.2.cloned.1.call-done = bf16[512,64]{0,1:T(8,128)(2,1)} async-done(((bf16[512,64]{0,1:T(8,128)(2,1)}), bf16[512,64]{0,1:T(8,128)(2,1)}) %all-reduce.2.cloned.1.call-update) | async-done | bytes 65552 | tf_op jit(solution)/shard_map/psum | solution.py:45
  122.1 2.4 %fusion.2 = bf16[512,256]{1,0:T(8,128)(2,1)} fusion(bf16[12,64,256]{2,1,0:T(8,128)(2,1)S(1)} %all_gather.7, s32[12,64]{1,0:T(8,128)S(1)} %add_select_fusion.1, s32[512]{0:T(512)S(1)} %select_reduce_fusion, pred[12,64]{1,0:T(8,128)(4,1)S(1)} %fusion.9, bf16[512,256]{1,0:T(8,128)(2,1)} %reduce-scatter.2.cloned.1.call-done, ...), kind=kOutput, calls=%fused_computation.7 | convolution fusion | flops 203030528 | bytes 990976 | tf_op jit(solution)/shard_map/dot_general | solution.py:47
  (12 shorter events, 0.3 us)
Async XLA Ops:
  7.4 1.6 %copy-start = (bf16[512,2048]{1,0:T(8,128)(2,1)S(1)}, bf16[512,2048]{1,0:T(8,128)(2,1)}, u32[]{:S(2)}) copy-start(bf16[512,2048]{1,0:T(8,128)(2,1)} %param.8) | copy-start | bytes 6291460
  7.4 74.9 %all-gather.2.cloned.1.call-start = ((), (), s32[]{:S(2)}) async-start(), calls=%async_computation.2 | async-start | bytes 3932160 | tf_op jit(solution)/shard_map/all_gather | solution.py:23
  8.1 6.7 %copy-start.3 = (s32[12]{0:T(128)S(1)}, s32[12]{0:T(128)}, u32[]{:S(2)}) copy-start(s32[12]{0:T(128)} %param.12) | copy-start | bytes 148
  8.1 14.7 %copy-start.5 = (s32[1,32]{1,0:T(1,128)S(1)}, s32[1,32]{1,0:T(1,128)}, u32[]{:S(2)}) copy-start(s32[1,32]{1,0:T(1,128)} %param.14) | copy-start | bytes 388
  8.1 14.7 %copy-start.4 = (s32[1,32]{1,0:T(1,128)S(1)}, s32[1,32]{1,0:T(1,128)}, u32[]{:S(2)}) copy-start(s32[1,32]{1,0:T(1,128)} %param.15) | copy-start | bytes 388
  8.1 15.1 %copy-start.1 = (s32[12]{0:T(128)S(1)}, s32[12]{0:T(128)}, u32[]{:S(2)}) copy-start(s32[12]{0:T(128)} %param.13) | copy-start | bytes 148
  8.1 20.2 %copy-start.2 = (bf16[3,64,256]{2,1,0:T(8,128)(2,1)S(1)}, bf16[3,64,256]{2,1,0:T(8,128)(2,1)}, u32[]{:S(2)}) copy-start(bf16[3,64,256]{2,1,0:T(8,128)(2,1)} %param.11) | copy-start | bytes 294916
  8.1 84.3 %reduce-scatter.2.cloned.1.call-start = ((), (), s32[]{:S(2)}) async-start(), calls=%async_computation.1 | async-start | bytes 1310720 | tf_op jit(solution)/shard_map/reduce_scatter | solution.py:26
  14.5 107.6 %all-reduce.2.cloned.1.call-start = ((), (), s32[]{:S(2)}) async-start(), calls=%async_computation.3 | async-start | bytes 131072 | tf_op jit(solution)/shard_map/psum | solution.py:45
Sparse Core Ops, SparseCore 0:
  9.8 72.3 all-gather.1
Sparse Core Ops, SparseCore 1:
  14.6 27.6 reduce-scatter.1
  92.5 29.6 all-reduce.1

commit v2 on v1

v2 whole, which is shorter than its diff:
```python
import functools

import jax
import jax.numpy as jnp
from jax import lax
from jax.experimental import pallas as pl
from jax.experimental.pallas import tpu as pltpu
from jax.sharding import PartitionSpec as P

MESH = pl.DeviceIdType.MESH
BF16 = jnp.bfloat16
F32 = jnp.float32


def kernel(
    n, width, rank_pad, adapters_here, chunks,
    tokens_hbm, weight_hbm, down_hbm, up_hbm, rank_ref, slot_ref, named_ref, lengths_ref,
    out_ref,
    tokens, weight, down, up, code, wide_sum, base, value_send, value_recv, shrink_send, shrink_recv,
    local_sem, right_sem, left_sem, line_sem, pair_send, pair_recv,
    value_ssem, value_rsem, shrink_ssem, shrink_rsem,
):
    part, me, mine = lax.axis_index("parts"), lax.axis_index("dp"), lax.axis_index("tensor")
    token_count = tokens.shape[0]
    unit = adapters_here * rank_pad
    half = unit // 2
    piece = half // chunks
    share = up.shape[2]
    has_left, has_right = me > 0, me < n - 1

    copies = [
        pltpu.make_async_copy(tokens_hbm, tokens, local_sem.at[0]),
        pltpu.make_async_copy(weight_hbm, weight, local_sem.at[1]),
        pltpu.make_async_copy(down_hbm, down.at[me], local_sem.at[2]),
        pltpu.make_async_copy(up_hbm, up.at[me], local_sem.at[3]),
    ]
    for copy in copies:
        copy.start()

    barrier = pltpu.get_barrier_semaphore()

    def greet(where):
        pl.semaphore_signal(barrier, inc=1, device_id=where, device_id_type=MESH)

    @pl.when(has_left)
    def _():
        greet((part, me - 1, mine))

    @pl.when(has_right)
    def _():
        greet((part, me + 1, mine))

    greet((1 - part, me, mine))
    for i in range(1, width):
        greet((part, me, lax.rem(mine + i, width)))

    inner = has_left & has_right

    @pl.when(inner)
    def _():
        pl.semaphore_wait(barrier, width + 2)

    @pl.when(jnp.logical_not(inner))
    def _():
        pl.semaphore_wait(barrier, width + 1)

    def rows_of(which, c):
        if c == chunks:
            return pl.ds(pl.multiple_of(which * half, half), half)
        return pl.ds(pl.multiple_of(which * half + c * piece, piece), piece)

    def place(u, which, c):
        return (up if c == chunks else down).at[u, rows_of(which, c)]

    def line(u, c, to, sems, own=False):
        source = (up_hbm if c == chunks else down_hbm).at[rows_of(part, c)] if own else place(u, part, c)
        return pltpu.make_async_remote_copy(
            src_ref=source, dst_ref=place(u, part, c), send_sem=sems.at[u, c],
            recv_sem=line_sem.at[u, c], device_id=(part, to, mine), device_id_type=MESH)

    def pair(u, c, which):
        return pltpu.make_async_remote_copy(
            src_ref=place(u, which, c), dst_ref=place(u, which, c), send_sem=pair_send.at[u, c],
            recv_sem=pair_recv.at[u, c], device_id=(1 - part, me, mine), device_id_type=MESH)

    for c in range(chunks + 1):
        @pl.when(has_right)
        def _():
            line(me, c, me + 1, right_sem, own=True).start()

        @pl.when(has_left)
        def _():
            line(me, c, me - 1, left_sem, own=True).start()

    copies[0].wait()
    copies[1].wait()

    def value_copy(peer):
        return pltpu.make_async_remote_copy(
            src_ref=value_send.at[peer], dst_ref=value_recv.at[mine], send_sem=value_ssem.at[peer],
            recv_sem=value_rsem.at[mine], device_id=(part, me, peer), device_id_type=MESH)

    def value_arrival(peer):
        return pltpu.make_async_remote_copy(
            src_ref=value_send.at[peer], dst_ref=value_recv.at[peer], send_sem=value_ssem.at[peer],
            recv_sem=value_rsem.at[peer], device_id=(part, me, peer), device_id_type=MESH)

    def block_product(owner):
        columns = pl.ds(pl.multiple_of(owner * share, share), share)
        return jnp.dot(tokens[...], weight[:, columns], preferred_element_type=F32).astype(BF16)

    @pl.loop(1, width)
    def _(i):
        peer = lax.rem(mine + i, width)
        value_send[peer] = block_product(peer)
        value_copy(peer).start()

    base[...] = block_product(mine).astype(F32)

    position = lax.broadcasted_iota(jnp.int32, (token_count, unit), 0)

    def visit(j, carry):
        start, values = carry
        row = slot_ref[named_ref[0, j]]
        mark = row * 8 + rank_ref[row]
        return start + lengths_ref[0, j], jnp.where(position >= start, mark, values)

    code[...] = lax.fori_loop(
        0, lengths_ref.shape[1], visit, (jnp.int32(0), jnp.zeros((token_count, unit), jnp.int32)))[1]

    column = lax.broadcasted_iota(jnp.int32, (token_count, unit), 1) // rank_pad

    def at_unit(u):
        return (code[...] >> 3) == column + u * adapters_here

    def unit_shrink(u):
        product = lax.dot_general(
            tokens[...], down[u], (((1,), (1,)), ((), ())), preferred_element_type=F32)
        return jnp.where(at_unit(u), product, 0.0)

    copies[2].wait()
    wide_sum[...] = unit_shrink(me)

    def sides(step):
        return ((me - step, me - 1, me + 1, me - step >= 0, has_right, right_sem),
                (me + step, me + 1, me - 1, me + step < n, has_left, left_sem))

    def pass_on(step):
        for c in range(chunks + 1):
            for u, source, onward, there, more, sems in sides(step):
                @pl.when(there)
                def _():
                    line(u, c, source, sems).wait_recv()

                    @pl.when(more)
                    def _():
                        line(u, c, onward, sems).start()

                    pair(u, c, part).start()

    def take(step):
        for u, source, onward, there, more, sems in sides(step):
            @pl.when(there)
            def _():
                for c in range(chunks):
                    pair(u, c, 1 - part).wait_recv()
                wide_sum[...] += unit_shrink(u)

    pass_on(1)

    @pl.loop(2, n)
    def _(step):
        pass_on(step)
        take(step - 1)

    @pl.loop(1, width)
    def _(i):
        peer = lax.rem(mine + i, width)
        value_arrival(peer).wait_recv()
        base[...] += value_recv[peer].astype(F32)

    take(n - 1)

    def selector(height, test):
        i = lax.broadcasted_iota(jnp.int32, (height, 2 * rank_pad), 0)
        j = lax.broadcasted_iota(jnp.int32, (height, 2 * rank_pad), 1)
        return jnp.where(test(i, j), 1.0, 0.0).astype(BF16)

    fold = selector(unit, lambda i, j: i % rank_pad == j % rank_pad)
    twice = jnp.dot(wide_sum[...].astype(BF16), fold, preferred_element_type=F32)
    middle = token_count // 2
    lane = lax.broadcasted_iota(jnp.int32, (middle, 2 * rank_pad), 1)
    packed = jnp.where(lane < rank_pad, twice[:middle], twice[middle:])
    shrink_send[...] = packed.astype(BF16)

    def shrink_copy(peer, slot):
        return pltpu.make_async_remote_copy(
            src_ref=shrink_send, dst_ref=shrink_recv.at[slot], send_sem=shrink_ssem.at[peer],
            recv_sem=shrink_rsem.at[slot], device_id=(part, me, peer), device_id_type=MESH)

    for i in range(1, width):
        shrink_copy(lax.rem(mine + i, width), mine).start()
    total = shrink_send[...].astype(F32)
    for i in range(1, width):
        peer = lax.rem(mine + i, width)
        shrink_copy(peer, peer).wait_recv()
        total = total + shrink_recv[peer].astype(F32)
    narrow = total.astype(BF16)
    first = selector(2 * rank_pad, lambda i, j: i == j % rank_pad)
    second = selector(2 * rank_pad, lambda i, j: i == j % rank_pad + rank_pad)
    spread = jnp.concatenate(
        [jnp.dot(narrow, first, preferred_element_type=F32),
         jnp.dot(narrow, second, preferred_element_type=F32)], axis=0)
    lane = lax.broadcasted_iota(jnp.int32, (token_count, 2 * rank_pad), 1) % rank_pad
    spread = jnp.where(lane < 16 * (code[:, : 2 * rank_pad] & 7), spread, 0.0)
    copies_of = -(-unit // (2 * rank_pad))
    tiled = jnp.concatenate([spread] * copies_of, axis=1)[:, :unit]

    copies[3].wait()

    def lift(u, total):
        @pl.when(u != me)
        def _():
            pair(u, chunks, 1 - part).wait_recv()
        chosen = jnp.where(at_unit(u), tiled, 0.0).astype(BF16)
        return total + jnp.dot(chosen, up[u], preferred_element_type=F32)

    update = lax.fori_loop(0, n, lift, jnp.zeros((token_count, share), F32))
    scale = 32.0 / (16 * (code[:, :1] & 7)).astype(F32)
    out_ref[...] = (base[...] + update * scale).astype(BF16)

    @pl.loop(0, n)
    def _(u):
        for c in range(chunks + 1):
            @pl.when((u <= me) & has_right)
            def _():
                line(u, c, me + 1, right_sem).wait_send()

            @pl.when((u >= me) & has_left)
            def _():
                line(u, c, me - 1, left_sem).wait_send()

            @pl.when(u != me)
            def _():
                pair(u, c, part).wait_send()

    for i in range(1, width):
        peer = lax.rem(mine + i, width)
        value_copy(peer).wait_send()
        shrink_copy(peer, mine).wait_send()


def local(n, width, tokens, value_weight, down_panels, up_panels, adapter_rank, adapter_slot, seg_adapter, seg_lengths):
    token_count, depth = tokens.shape
    adapters_here, rank_pad, _ = down_panels.shape
    share = up_panels.shape[2]
    unit = adapters_here * rank_pad
    chunks = 3 if n <= 8 else 1
    dma = pltpu.SemaphoreType.DMA
    hbm = pl.BlockSpec(memory_space=pl.ANY)
    smem = pl.BlockSpec(memory_space=pltpu.SMEM)
    return pl.pallas_call(
        functools.partial(kernel, n, width, rank_pad, adapters_here, chunks),
        out_shape=jax.ShapeDtypeStruct((token_count, share), BF16),
        in_specs=[hbm] * 4 + [smem] * 4,
        out_specs=pl.BlockSpec(memory_space=pltpu.VMEM),
        scratch_shapes=[
            pltpu.VMEM(tokens.shape, BF16),
            pltpu.VMEM(value_weight.shape, BF16),
            pltpu.VMEM((n, unit, depth), BF16),
            pltpu.VMEM((n, unit, share), BF16),
            pltpu.VMEM((token_count, unit), jnp.int32),
            pltpu.VMEM((token_count, unit), F32),
            pltpu.VMEM((token_count, share), F32),
            pltpu.VMEM((width, token_count, share), BF16),
            pltpu.VMEM((width, token_count, share), BF16),
            pltpu.VMEM((token_count // 2, 2 * rank_pad), BF16),
            pltpu.VMEM((width, token_count // 2, 2 * rank_pad), BF16),
            dma((4,)),
            dma((n, chunks + 1)),
            dma((n, chunks + 1)),
            dma((n, chunks + 1)),
            dma((n, chunks + 1)),
            dma((n, chunks + 1)),
            dma((width,)),
            dma((width,)),
            dma((width,)),
            dma((width,)),
        ],
        compiler_params=pltpu.CompilerParams(
            collective_id=0, has_side_effects=True, vmem_limit_bytes=50 * 1024 * 1024),
    )(tokens, value_weight, down_panels.reshape(unit, depth), up_panels.reshape(unit, share),
      adapter_rank, adapter_slot, seg_adapter, seg_lengths)


def solution(mesh):
    return jax.shard_map(
        functools.partial(local, mesh.shape["dp"], mesh.shape["tensor"]),
        mesh=mesh,
        in_specs=(
            P(("parts", "dp"), "tensor"),
            P("tensor", None),
            P("dp", None, "tensor"),
            P("dp", None, "tensor"),
            P(),
            P("parts"),
            P(("parts", "dp"), None),
            P(("parts", "dp"), None),
        ),
        out_specs=P(("parts", "dp"), "tensor"),
        check_vma=False,
    )
```

time: 132 us -> 55.7 us (0.42)
  waiting for transfers between devices: 59.9 us -> 0 us
  Pallas kernels: 0 us -> 48.4 us
  blocking collectives: 21.3 us -> 0 us
  other arithmetic: 17.4 us -> 0 us
  between operations: 15 us -> 0.02 us
  matrix products: 12.8 us -> 0 us
  local copies, waits for them, and re-layouts: 5.36 us -> 6.94 us
    pallas_call x0 -> x1, Pallas kernels: none -> 48.4 us  [local(): pl.pallas_call(functools.partial(kernel, n, width, rank_pad, adapters_her...]
    psum x1 -> x0, waiting for transfers between devices: 29.7 us -> none  [local(): summed = lax.psum(shrink.astype(jnp.bfloat16), 'tensor')]
    all_gather x1 -> x0, waiting for transfers between devices: 29.5 us -> none  [local(): down_all = lax.all_gather(down_panels, 'dp', axis=0, tiled=True)]
    all_gather x1 -> x0, blocking collectives: 21.3 us -> none  [local(): up_all = lax.all_gather(up_panels, 'dp', axis=0, tiled=True)]
    dot_general x3 -> x0, matrix products: 12.8 us -> none  [the longest x1 5.54 us: local(): jnp.dot(tokens, value_weight, preferred_element_type=jnp.float32)]
    gather x9 -> x0, other arithmetic: 8.8 us -> none  [the longest x6 4.46 us: local(): column_keep = column % rank_pad < 16 * adapter_rank[column_row]]
    unnamed x12 -> x15, local copies, waits for them, and re-layouts: 0.79 us -> 6.94 us
    lt x2 -> x0, other arithmetic: 3.1 us -> none  [local(): column_keep = column % rank_pad < 16 * adapter_rank[column_row]]
  transfers between devices with their start and end apart: 3 -> 0, of which waited for: 2 -> 0; matrix products, arithmetic and copies ran while one was open for 25% -> 0% of each run, Pallas kernels for 0% -> 0%
where the time goes in v2:
time: 55.7 us; the launch traced here: 55.4 us
  Pallas kernels  48.4 us (87%)
  local copies, waits for them, and re-layouts  6.94 us (12%)
    pallas_call x1, Pallas kernels, local(): pl.pallas_call(functools.partial(kernel, n, width, rank_pad, adapters_her...  48.4 us
    unnamed x15, local copies, waits for them, and re-layouts  6.94 us

profile of v2, /device:TPU:0, one launch (start us, length us, event | category | flops | bytes accessed | tf_op | source)
XLA Modules:
  0.0 55.4 jit_solution(18211770637423975316)
XLA Ops:
  0.0 0.0 copy-start
  0.0 1.6 %copy-done = bf16[512,2048]{1,0:T(8,128)(2,1)S(1)} copy-done((bf16[512,2048]{1,0:T(8,128)(2,1)S(1)}, bf16[512,2048]{1,0:T(8,128)(2,1)}, u32[]{:S(2)}) %copy-start) | copy-done | bytes 2097176
  1.6 0.0 copy-start.1
  1.6 1.1 %copy-done.1 = bf16[3,64,2048]{2,1,0:T(8,128)(2,1)S(1)} copy-done((bf16[3,64,2048]{2,1,0:T(8,128)(2,1)S(1)}, bf16[3,64,2048]{2,1,0:T(8,128)(2,1)}, u32[]{:S(2)}) %copy-start.1) | copy-done | bytes 786456
  2.7 0.0 copy-start.2
  2.7 0.9 %copy-done.2 = bf16[3,64,256]{2,1,0:T(8,128)(2,1)S(1)} copy-done((bf16[3,64,256]{2,1,0:T(8,128)(2,1)S(1)}, bf16[3,64,256]{2,1,0:T(8,128)(2,1)}, u32[]{:S(2)}) %copy-start.2) | copy-done | bytes 98328
  3.6 0.0 copy-start.3
  3.6 0.7 %copy-done.3 = s32[12]{0:T(128)S(1)} copy-done((s32[12]{0:T(128)S(1)}, s32[12]{0:T(128)}, u32[]{:S(2)}) %copy-start.3) | copy-done | bytes 72
  4.3 0.0 copy-start.4
  4.3 0.7 %copy-done.4 = s32[12]{0:T(128)S(1)} copy-done((s32[12]{0:T(128)S(1)}, s32[12]{0:T(128)}, u32[]{:S(2)}) %copy-start.4) | copy-done | bytes 72
  4.9 0.0 copy-start.5
  4.9 0.7 %copy-done.5 = s32[1,32]{1,0:T(1,128)S(1)} copy-done((s32[1,32]{1,0:T(1,128)S(1)}, s32[1,32]{1,0:T(1,128)}, u32[]{:S(2)}) %copy-start.5) | copy-done | bytes 152
  5.6 0.0 copy-start.6
  5.6 0.7 %copy-done.6 = s32[1,32]{1,0:T(1,128)S(1)} copy-done((s32[1,32]{1,0:T(1,128)S(1)}, s32[1,32]{1,0:T(1,128)}, u32[]{:S(2)}) %copy-start.6) | copy-done | bytes 152
  6.2 48.4 %shard_map.82 = bf16[512,256]{1,0:T(8,128)(2,1)S(1)} custom-call(bf16[512,2048]{1,0:T(8,128)(2,1)S(1)} %copy-done, bf16[2048,1024]{1,0:T(8,128)(2,1)} %weight_hbm.1, bf16[192,2048]{1,0:T(8,128)(2,1)S(1)} %bitcast.2, bf16[192,256]{1,0:T(8,128)(2,1)S(1)} %bitcast.3, s32[12]{0:T(128)S(1)} %copy-done.3, s32[12]{0:T(128)S(1)} %copy-done.4, ...), custom_call_target="tpu_custom_call" | custom-call | tf_op jit(solution)/shard_map/pallas_call | solution.py:262
  54.7 0.7 %copy.10 = bf16[512,256]{1,0:T(8,128)(2,1)} copy(bf16[512,256]{1,0:T(8,128)(2,1)S(1)} %shard_map.82) | data formatting | bytes 524288
Async XLA Ops:
  0.0 1.6 %copy-start = (bf16[512,2048]{1,0:T(8,128)(2,1)S(1)}, bf16[512,2048]{1,0:T(8,128)(2,1)}, u32[]{:S(2)}) copy-start(bf16[512,2048]{1,0:T(8,128)(2,1)} %tokens_hbm.1) | copy-start | bytes 6291460
  1.6 1.1 %copy-start.1 = (bf16[3,64,2048]{2,1,0:T(8,128)(2,1)S(1)}, bf16[3,64,2048]{2,1,0:T(8,128)(2,1)}, u32[]{:S(2)}) copy-start(bf16[3,64,2048]{2,1,0:T(8,128)(2,1)} %param.10) | copy-start | bytes 2359300
  2.7 0.9 %copy-start.2 = (bf16[3,64,256]{2,1,0:T(8,128)(2,1)S(1)}, bf16[3,64,256]{2,1,0:T(8,128)(2,1)}, u32[]{:S(2)}) copy-start(bf16[3,64,256]{2,1,0:T(8,128)(2,1)} %param.11) | copy-start | bytes 294916
  3.6 0.7 %copy-start.3 = (s32[12]{0:T(128)S(1)}, s32[12]{0:T(128)}, u32[]{:S(2)}) copy-start(s32[12]{0:T(128)} %rank_ref.1) | copy-start | bytes 148
  4.3 0.7 %copy-start.4 = (s32[12]{0:T(128)S(1)}, s32[12]{0:T(128)}, u32[]{:S(2)}) copy-start(s32[12]{0:T(128)} %slot_ref.1) | copy-start | bytes 148
  4.9 0.7 %copy-start.5 = (s32[1,32]{1,0:T(1,128)S(1)}, s32[1,32]{1,0:T(1,128)}, u32[]{:S(2)}) copy-start(s32[1,32]{1,0:T(1,128)} %named_ref.1) | copy-start | bytes 388
  5.6 0.7 %copy-start.6 = (s32[1,32]{1,0:T(1,128)S(1)}, s32[1,32]{1,0:T(1,128)}, u32[]{:S(2)}) copy-start(s32[1,32]{1,0:T(1,128)} %lengths_ref.1) | copy-start | bytes 388

commit v3 on v2

--- a/solution.py
+++ b/solution.py
@@ -13,9 +13,10 @@
 
 
 def kernel(
-    n, width, rank_pad, adapters_here, chunks,
-    tokens_hbm, weight_hbm, down_hbm, up_hbm, rank_ref, slot_ref, named_ref, lengths_ref,
+    n, width, rank_pad, adapters_here, chunks, window,
+    tokens_hbm, weight_hbm, down_hbm, up_hbm, rank_hbm, slot_hbm, named_hbm, lengths_hbm,
     out_ref,
+    rank_ref, slot_ref, named_ref, lengths_ref,
     tokens, weight, down, up, code, wide_sum, base, value_send, value_recv, shrink_send, shrink_recv,
     local_sem, right_sem, left_sem, line_sem, pair_send, pair_recv,
     value_ssem, value_rsem, shrink_ssem, shrink_rsem,
@@ -33,6 +34,10 @@
         pltpu.make_async_copy(weight_hbm, weight, local_sem.at[1]),
         pltpu.make_async_copy(down_hbm, down.at[me], local_sem.at[2]),
         pltpu.make_async_copy(up_hbm, up.at[me], local_sem.at[3]),
+        pltpu.make_async_copy(rank_hbm, rank_ref, local_sem.at[4]),
+        pltpu.make_async_copy(slot_hbm, slot_ref, local_sem.at[5]),
+        pltpu.make_async_copy(named_hbm, named_ref, local_sem.at[6]),
+        pltpu.make_async_copy(lengths_hbm, lengths_ref, local_sem.at[7]),
     ]
     for copy in copies:
         copy.start()
@@ -83,14 +88,16 @@
             src_ref=place(u, which, c), dst_ref=place(u, which, c), send_sem=pair_send.at[u, c],
             recv_sem=pair_recv.at[u, c], device_id=(1 - part, me, mine), device_id_type=MESH)
 
-    for c in range(chunks + 1):
-        @pl.when(has_right)
-        def _():
-            line(me, c, me + 1, right_sem, own=True).start()
-
-        @pl.when(has_left)
-        def _():
-            line(me, c, me - 1, left_sem, own=True).start()
+    def send_own(c):
+        for to, there, sems in ((me + 1, has_right, right_sem), (me - 1, has_left, left_sem)):
+            @pl.when(there)
+            def _():
+                if window <= c < chunks:
+                    line(me, c - window, to, sems).wait_send()
+                line(me, c, to, sems, own=True).start()
+
+    for c in range(min(window, chunks)):
+        send_own(c)
 
     copies[0].wait()
     copies[1].wait()
@@ -115,6 +122,8 @@
         value_send[peer] = block_product(peer)
         value_copy(peer).start()
 
+    for c in range(window, chunks):
+        send_own(c)
     base[...] = block_product(mine).astype(F32)
 
     position = lax.broadcasted_iota(jnp.int32, (token_count, unit), 0)
@@ -125,6 +134,8 @@
         mark = row * 8 + rank_ref[row]
         return start + lengths_ref[0, j], jnp.where(position >= start, mark, values)
 
+    for copy in copies[4:]:
+        copy.wait()
     code[...] = lax.fori_loop(
         0, lengths_ref.shape[1], visit, (jnp.int32(0), jnp.zeros((token_count, unit), jnp.int32)))[1]
 
@@ -145,8 +156,8 @@
         return ((me - step, me - 1, me + 1, me - step >= 0, has_right, right_sem),
                 (me + step, me + 1, me - 1, me + step < n, has_left, left_sem))
 
-    def pass_on(step):
-        for c in range(chunks + 1):
+    def pass_on(step, pieces):
+        for c in pieces:
             for u, source, onward, there, more, sems in sides(step):
                 @pl.when(there)
                 def _():
@@ -154,6 +165,9 @@
 
                     @pl.when(more)
                     def _():
+                        if c < chunks:
+                            before = u if c >= window else u + me - source
+                            line(before, (c - window) % chunks, onward, sems).wait_send()
                         line(u, c, onward, sems).start()
 
                     pair(u, c, part).start()
@@ -166,11 +180,11 @@
                     pair(u, c, 1 - part).wait_recv()
                 wide_sum[...] += unit_shrink(u)
 
-    pass_on(1)
+    pass_on(1, range(chunks))
 
     @pl.loop(2, n)
     def _(step):
-        pass_on(step)
+        pass_on(step, range(chunks))
         take(step - 1)
 
     @pl.loop(1, width)
@@ -200,6 +214,12 @@
 
     for i in range(1, width):
         shrink_copy(lax.rem(mine + i, width), mine).start()
+    send_own(chunks)
+
+    @pl.loop(1, n)
+    def _(step):
+        pass_on(step, [chunks])
+
     total = shrink_send[...].astype(F32)
     for i in range(1, width):
         peer = lax.rem(mine + i, width)
@@ -232,13 +252,16 @@
     @pl.loop(0, n)
     def _(u):
         for c in range(chunks + 1):
-            @pl.when((u <= me) & has_right)
-            def _():
-                line(u, c, me + 1, right_sem).wait_send()
-
-            @pl.when((u >= me) & has_left)
-            def _():
-                line(u, c, me - 1, left_sem).wait_send()
+            if c >= chunks - window:
+                first = c == chunks
+
+                @pl.when((u <= me if first else u == 0) & has_right)
+                def _():
+                    line(u, c, me + 1, right_sem).wait_send()
+
+                @pl.when((u >= me if first else u == n - 1) & has_left)
+                def _():
+                    line(u, c, me - 1, left_sem).wait_send()
 
             @pl.when(u != me)
             def _():
@@ -255,16 +278,19 @@
     adapters_here, rank_pad, _ = down_panels.shape
     share = up_panels.shape[2]
     unit = adapters_here * rank_pad
-    chunks = 3 if n <= 8 else 1
+    chunks, window = (3, 2) if n <= 8 else (1, 1)
     dma = pltpu.SemaphoreType.DMA
-    hbm = pl.BlockSpec(memory_space=pl.ANY)
-    smem = pl.BlockSpec(memory_space=pltpu.SMEM)
+    hbm = pl.BlockSpec(memory_space=pltpu.HBM)
     return pl.pallas_call(
-        functools.partial(kernel, n, width, rank_pad, adapters_here, chunks),
+        functools.partial(kernel, n, width, rank_pad, adapters_here, chunks, window),
         out_shape=jax.ShapeDtypeStruct((token_count, share), BF16),
-        in_specs=[hbm] * 4 + [smem] * 4,
+        in_specs=[hbm] * 8,
         out_specs=pl.BlockSpec(memory_space=pltpu.VMEM),
         scratch_shapes=[
+            pltpu.SMEM(adapter_rank.shape, jnp.int32),
+            pltpu.SMEM(adapter_slot.shape, jnp.int32),
+            pltpu.SMEM(seg_adapter.shape, jnp.int32),
+            pltpu.SMEM(seg_lengths.shape, jnp.int32),
             pltpu.VMEM(tokens.shape, BF16),
             pltpu.VMEM(value_weight.shape, BF16),
             pltpu.VMEM((n, unit, depth), BF16),
@@ -276,7 +302,7 @@
             pltpu.VMEM((width, token_count, share), BF16),
             pltpu.VMEM((token_count // 2, 2 * rank_pad), BF16),
             pltpu.VMEM((width, token_count // 2, 2 * rank_pad), BF16),
-            dma((4,)),
+            dma((8,)),
             dma((n, chunks + 1)),
             dma((n, chunks + 1)),
             dma((n, chunks + 1)),
@@ -288,7 +314,7 @@
             dma((width,)),
         ],
         compiler_params=pltpu.CompilerParams(
-            collective_id=0, has_side_effects=True, vmem_limit_bytes=50 * 1024 * 1024),
+            collective_id=0, has_side_effects=True, vmem_limit_bytes=62 * 1024 * 1024),
     )(tokens, value_weight, down_panels.reshape(unit, depth), up_panels.reshape(unit, share),
       adapter_rank, adapter_slot, seg_adapter, seg_lengths)
 

time: 55.7 us -> 57.1 us (1.025)
  Pallas kernels: 48.4 us -> 55.3 us
  local copies, waits for them, and re-layouts: 6.94 us -> 1.67 us
    pallas_call x1, Pallas kernels: 48.4 us -> 55.3 us  [local(): pl.pallas_call(functools.partial(kernel, n, width, rank_pad, adapters_her...]
    unnamed x15 -> x1, local copies, waits for them, and re-layouts: 6.94 us -> 1.67 us
where the time goes in v3:
time: 57.1 us; the launch traced here: 56.9 us
  Pallas kernels  55.3 us (97%)
  local copies, waits for them, and re-layouts  1.67 us (3%)
    pallas_call x1, Pallas kernels, local(): pl.pallas_call(functools.partial(kernel, n, width, rank_pad, adapters_her...  55.3 us
    unnamed x1, local copies, waits for them, and re-layouts  1.67 us

profile of v3, /device:TPU:0, one launch (start us, length us, event | category | flops | bytes accessed | tf_op | source)
XLA Modules:
  0.0 56.9 jit_solution(785918212241544996)
XLA Ops:
  0.0 55.3 %shard_map.82 = bf16[512,256]{1,0:T(8,128)(2,1)} custom-call(bf16[512,2048]{1,0:T(8,128)(2,1)} %tokens_hbm.1, bf16[2048,1024]{1,0:T(8,128)(2,1)} %weight_hbm.1, bf16[192,2048]{1,0:T(8,128)(2,1)} %bitcast.2, bf16[192,256]{1,0:T(8,128)(2,1)} %bitcast.3, s32[12]{0:T(128)} %rank_hbm.1, s32[12]{0:T(128)} %slot_hbm.1, s32[1,32]{1,0:T(1,128)} %named_hbm.1, ...), custom_call_target="tpu_custom_call" | custom-call | tf_op jit(solution)/shard_map/pallas_call | solution.py:284
  55.3 1.7 %copy.10 = bf16[512,256]{1,0:T(8,128)(2,1)} copy(bf16[512,256]{1,0:T(8,128)(2,1)} %shard_map.82) | data formatting | bytes 524288

commit v4 on v3

--- a/solution.py
+++ b/solution.py
@@ -92,11 +92,12 @@
         for to, there, sems in ((me + 1, has_right, right_sem), (me - 1, has_left, left_sem)):
             @pl.when(there)
             def _():
-                if window <= c < chunks:
+                if window and window <= c < chunks:
                     line(me, c - window, to, sems).wait_send()
                 line(me, c, to, sems, own=True).start()
 
-    for c in range(min(window, chunks)):
+    first_pieces = min(window or chunks, chunks)
+    for c in range(first_pieces):
         send_own(c)
 
     copies[0].wait()
@@ -122,7 +123,7 @@
         value_send[peer] = block_product(peer)
         value_copy(peer).start()
 
-    for c in range(window, chunks):
+    for c in range(first_pieces, chunks):
         send_own(c)
     base[...] = block_product(mine).astype(F32)
 
@@ -165,7 +166,7 @@
 
                     @pl.when(more)
                     def _():
-                        if c < chunks:
+                        if window and c < chunks:
                             before = u if c >= window else u + me - source
                             line(before, (c - window) % chunks, onward, sems).wait_send()
                         line(u, c, onward, sems).start()
@@ -181,10 +182,12 @@
                 wide_sum[...] += unit_shrink(u)
 
     pass_on(1, range(chunks))
+    send_own(chunks)
 
     @pl.loop(2, n)
     def _(step):
         pass_on(step, range(chunks))
+        pass_on(step - 1, [chunks])
         take(step - 1)
 
     @pl.loop(1, width)
@@ -214,12 +217,7 @@
 
     for i in range(1, width):
         shrink_copy(lax.rem(mine + i, width), mine).start()
-    send_own(chunks)
-
-    @pl.loop(1, n)
-    def _(step):
-        pass_on(step, [chunks])
-
+    pass_on(n - 1, [chunks])
     total = shrink_send[...].astype(F32)
     for i in range(1, width):
         peer = lax.rem(mine + i, width)
@@ -252,8 +250,8 @@
     @pl.loop(0, n)
     def _(u):
         for c in range(chunks + 1):
-            if c >= chunks - window:
-                first = c == chunks
+            if not window or c >= chunks - window:
+                first = c == chunks or not window
 
                 @pl.when((u <= me if first else u == 0) & has_right)
                 def _():
@@ -278,7 +276,7 @@
     adapters_here, rank_pad, _ = down_panels.shape
     share = up_panels.shape[2]
     unit = adapters_here * rank_pad
-    chunks, window = (3, 2) if n <= 8 else (1, 1)
+    chunks, window = (3, 0) if n <= 8 else (1, 0)
     dma = pltpu.SemaphoreType.DMA
     hbm = pl.BlockSpec(memory_space=pltpu.HBM)
     return pl.pallas_call(

time: 57.1 us -> 49.9 us (0.87)
  Pallas kernels: 55.3 us -> 48 us
    pallas_call x1, Pallas kernels: 55.3 us -> 48 us  [local(): pl.pallas_call(functools.partial(kernel, n, width, rank_pad, adapters_her...]
where the time goes in v4:
time: 49.9 us; the launch traced here: 49.6 us
  Pallas kernels  48 us (96%)
  local copies, waits for them, and re-layouts  1.67 us (3%)
    pallas_call x1, Pallas kernels, local(): pl.pallas_call(functools.partial(kernel, n, width, rank_pad, adapters_her...  48 us
    unnamed x1, local copies, waits for them, and re-layouts  1.67 us

profile of v4, /device:TPU:0, one launch (start us, length us, event | category | flops | bytes accessed | tf_op | source)
XLA Modules:
  0.0 49.6 jit_solution(14317835416405251139)
XLA Ops:
  0.0 48.0 %shard_map.82 = bf16[512,256]{1,0:T(8,128)(2,1)} custom-call(bf16[512,2048]{1,0:T(8,128)(2,1)} %tokens_hbm.1, bf16[2048,1024]{1,0:T(8,128)(2,1)} %weight_hbm.1, bf16[192,2048]{1,0:T(8,128)(2,1)} %bitcast.2, bf16[192,256]{1,0:T(8,128)(2,1)} %bitcast.3, s32[12]{0:T(128)} %rank_hbm.1, s32[12]{0:T(128)} %slot_hbm.1, s32[1,32]{1,0:T(1,128)} %named_hbm.1, ...), custom_call_target="tpu_custom_call" | custom-call | tf_op jit(solution)/shard_map/pallas_call | solution.py:282
  48.0 1.7 %copy.10 = bf16[512,256]{1,0:T(8,128)(2,1)} copy(bf16[512,256]{1,0:T(8,128)(2,1)} %shard_map.82) | data formatting | bytes 524288

commit v5 on v4

--- a/solution.py
+++ b/solution.py
@@ -70,6 +70,8 @@
         pl.semaphore_wait(barrier, width + 1)
 
     def rows_of(which, c):
+        if c == chunks + 1:
+            which, c = 1 - which, chunks - 1
         if c == chunks:
             return pl.ds(pl.multiple_of(which * half, half), half)
         return pl.ds(pl.multiple_of(which * half + c * piece, piece), piece)
@@ -92,13 +94,15 @@
         for to, there, sems in ((me + 1, has_right, right_sem), (me - 1, has_left, left_sem)):
             @pl.when(there)
             def _():
-                if window and window <= c < chunks:
-                    line(me, c - window, to, sems).wait_send()
                 line(me, c, to, sems, own=True).start()
 
     first_pieces = min(window or chunks, chunks)
     for c in range(first_pieces):
         send_own(c)
+
+    @pl.when((me == 0) | (me == n - 1))
+    def _():
+        send_own(chunks + 1)
 
     copies[0].wait()
     copies[1].wait()
@@ -154,39 +158,46 @@
     wide_sum[...] = unit_shrink(me)
 
     def sides(step):
-        return ((me - step, me - 1, me + 1, me - step >= 0, has_right, right_sem),
-                (me + step, me + 1, me - 1, me + step < n, has_left, left_sem))
+        return ((me - step, me - 1, me + 1, me - step >= 0, has_right, right_sem, me == step),
+                (me + step, me + 1, me - 1, me + step < n, has_left, left_sem, me + step == n - 1))
 
     def pass_on(step, pieces):
         for c in pieces:
-            for u, source, onward, there, more, sems in sides(step):
-                @pl.when(there)
+            for u, source, onward, there, more, sems, end in sides(step):
+                @pl.when(there & end if c == chunks + 1 else there)
                 def _():
                     line(u, c, source, sems).wait_recv()
 
                     @pl.when(more)
                     def _():
-                        if window and c < chunks:
-                            before = u if c >= window else u + me - source
-                            line(before, (c - window) % chunks, onward, sems).wait_send()
                         line(u, c, onward, sems).start()
 
-                    pair(u, c, part).start()
+                    if c == chunks - 1:
+                        @pl.when(jnp.logical_not(end))
+                        def _():
+                            pair(u, c, part).start()
+                    elif c <= chunks:
+                        pair(u, c, part).start()
 
     def take(step):
-        for u, source, onward, there, more, sems in sides(step):
+        for u, source, onward, there, more, sems, end in sides(step):
             @pl.when(there)
             def _():
-                for c in range(chunks):
+                for c in range(chunks - 1):
                     pair(u, c, 1 - part).wait_recv()
+
+                @pl.when(jnp.logical_not(end))
+                def _():
+                    pair(u, chunks - 1, 1 - part).wait_recv()
                 wide_sum[...] += unit_shrink(u)
 
-    pass_on(1, range(chunks))
+    down_pieces = [*range(chunks), chunks + 1]
+    pass_on(1, down_pieces)
     send_own(chunks)
 
     @pl.loop(2, n)
     def _(step):
-        pass_on(step, range(chunks))
+        pass_on(step, down_pieces)
         pass_on(step - 1, [chunks])
         take(step - 1)
 
@@ -261,9 +272,17 @@
                 def _():
                     line(u, c, me - 1, left_sem).wait_send()
 
-            @pl.when(u != me)
+            @pl.when((u != me) & (u != 0) & (u != n - 1) if c == chunks - 1 else u != me)
             def _():
                 pair(u, c, part).wait_send()
+
+    @pl.when(has_right)
+    def _():
+        line(0, chunks + 1, me + 1, right_sem).wait_send()
+
+    @pl.when(has_left)
+    def _():
+        line(n - 1, chunks + 1, me - 1, left_sem).wait_send()
 
     for i in range(1, width):
         peer = lax.rem(mine + i, width)
@@ -301,11 +320,11 @@
             pltpu.VMEM((token_count // 2, 2 * rank_pad), BF16),
             pltpu.VMEM((width, token_count // 2, 2 * rank_pad), BF16),
             dma((8,)),
-            dma((n, chunks + 1)),
-            dma((n, chunks + 1)),
-            dma((n, chunks + 1)),
-            dma((n, chunks + 1)),
-            dma((n, chunks + 1)),
+            dma((n, chunks + 2)),
+            dma((n, chunks + 2)),
+            dma((n, chunks + 2)),
+            dma((n, chunks + 2)),
+            dma((n, chunks + 2)),
             dma((width,)),
             dma((width,)),
             dma((width,)),

time: 49.9 us -> 46.9 us (0.940)
  Pallas kernels: 48 us -> 44.9 us
    pallas_call x1, Pallas kernels: 48 us -> 44.9 us  [local(): pl.pallas_call(functools.partial(kernel, n, width, rank_pad, adapters_her...]
where the time goes in v5:
time: 46.9 us; the launch traced here: 46.6 us
  Pallas kernels  44.9 us (96%)
  local copies, waits for them, and re-layouts  1.67 us (4%)
    pallas_call x1, Pallas kernels, local(): pl.pallas_call(functools.partial(kernel, n, width, rank_pad, adapters_her...  44.9 us
    unnamed x1, local copies, waits for them, and re-layouts  1.67 us

profile of v5, /device:TPU:0, one launch (start us, length us, event | category | flops | bytes accessed | tf_op | source)
XLA Modules:
  0.0 46.6 jit_solution(12226452431485977982)
XLA Ops:
  0.0 44.9 %shard_map.82 = bf16[512,256]{1,0:T(8,128)(2,1)} custom-call(bf16[512,2048]{1,0:T(8,128)(2,1)} %tokens_hbm.1, bf16[2048,1024]{1,0:T(8,128)(2,1)} %weight_hbm.1, bf16[192,2048]{1,0:T(8,128)(2,1)} %bitcast.2, bf16[192,256]{1,0:T(8,128)(2,1)} %bitcast.3, s32[12]{0:T(128)} %rank_hbm.1, s32[12]{0:T(128)} %slot_hbm.1, s32[1,32]{1,0:T(1,128)} %named_hbm.1, ...), custom_call_target="tpu_custom_call" | custom-call | tf_op jit(solution)/shard_map/pallas_call | solution.py:301
  44.9 1.7 %copy.10 = bf16[512,256]{1,0:T(8,128)(2,1)} copy(bf16[512,256]{1,0:T(8,128)(2,1)} %shard_map.82) | data formatting | bytes 524288

commit v6 on v5

--- a/solution.py
+++ b/solution.py
@@ -193,12 +193,21 @@
 
     down_pieces = [*range(chunks), chunks + 1]
     pass_on(1, down_pieces)
-    send_own(chunks)
+    if n == 2:
+        send_own(chunks)
 
     @pl.loop(2, n)
     def _(step):
         pass_on(step, down_pieces)
-        pass_on(step - 1, [chunks])
+
+        @pl.when(step == 2)
+        def _():
+            send_own(chunks)
+
+        @pl.when(step > 2)
+        def _():
+            pass_on(step - 2, [chunks])
+
         take(step - 1)
 
     @pl.loop(1, width)
@@ -228,7 +237,8 @@
 
     for i in range(1, width):
         shrink_copy(lax.rem(mine + i, width), mine).start()
-    pass_on(n - 1, [chunks])
+    for step in range(max(1, n - 2), n):
+        pass_on(step, [chunks])
     total = shrink_send[...].astype(F32)
     for i in range(1, width):
         peer = lax.rem(mine + i, width)

time: 46.9 us -> 46.1 us (0.983)
  Pallas kernels: 44.9 us -> 43.9 us
    pallas_call x1, Pallas kernels: 44.9 us -> 43.9 us  [local(): pl.pallas_call(functools.partial(kernel, n, width, rank_pad, adapters_her...]
where the time goes in v6:
time: 46.1 us; the launch traced here: 45.5 us
  Pallas kernels  43.9 us (95%)
  local copies, waits for them, and re-layouts  1.67 us (4%)
    pallas_call x1, Pallas kernels, local(): pl.pallas_call(functools.partial(kernel, n, width, rank_pad, adapters_her...  43.9 us
    unnamed x1, local copies, waits for them, and re-layouts  1.67 us

profile of v6, /device:TPU:0, one launch (start us, length us, event | category | flops | bytes accessed | tf_op | source)
XLA Modules:
  0.0 45.5 jit_solution(8591870019232272950)
XLA Ops:
  0.0 43.9 %shard_map.82 = bf16[512,256]{1,0:T(8,128)(2,1)} custom-call(bf16[512,2048]{1,0:T(8,128)(2,1)} %tokens_hbm.1, bf16[2048,1024]{1,0:T(8,128)(2,1)} %weight_hbm.1, bf16[192,2048]{1,0:T(8,128)(2,1)} %bitcast.2, bf16[192,256]{1,0:T(8,128)(2,1)} %bitcast.3, s32[12]{0:T(128)} %rank_hbm.1, s32[12]{0:T(128)} %slot_hbm.1, s32[1,32]{1,0:T(1,128)} %named_hbm.1, ...), custom_call_target="tpu_custom_call" | custom-call | tf_op jit(solution)/shard_map/pallas_call | solution.py:311
  43.9 1.7 %copy.10 = bf16[512,256]{1,0:T(8,128)(2,1)} copy(bf16[512,256]{1,0:T(8,128)(2,1)} %shard_map.82) | data formatting | bytes 524288

commit v7 on v6

--- a/solution.py
+++ b/solution.py
@@ -39,9 +39,6 @@
         pltpu.make_async_copy(named_hbm, named_ref, local_sem.at[6]),
         pltpu.make_async_copy(lengths_hbm, lengths_ref, local_sem.at[7]),
     ]
-    for copy in copies:
-        copy.start()
-
     barrier = pltpu.get_barrier_semaphore()
 
     def greet(where):
@@ -103,6 +100,9 @@
     @pl.when((me == 0) | (me == n - 1))
     def _():
         send_own(chunks + 1)
+
+    for copy in copies:
+        copy.start()
 
     copies[0].wait()
     copies[1].wait()

time: 46.1 us -> 47.5 us (1.030)
  Pallas kernels: 43.9 us -> 45.3 us
    pallas_call x1, Pallas kernels: 43.9 us -> 45.3 us  [local(): pl.pallas_call(functools.partial(kernel, n, width, rank_pad, adapters_her...]
where the time goes in v7:
time: 47.5 us; the launch traced here: 47 us
  Pallas kernels  45.3 us (95%)
  local copies, waits for them, and re-layouts  1.67 us (4%)
    pallas_call x1, Pallas kernels, local(): pl.pallas_call(functools.partial(kernel, n, width, rank_pad, adapters_her...  45.3 us
    unnamed x1, local copies, waits for them, and re-layouts  1.67 us

profile of v7, /device:TPU:0, one launch (start us, length us, event | category | flops | bytes accessed | tf_op | source)
XLA Modules:
  0.0 47.0 jit_solution(2752170198705529012)
XLA Ops:
  0.0 45.3 %shard_map.82 = bf16[512,256]{1,0:T(8,128)(2,1)} custom-call(bf16[512,2048]{1,0:T(8,128)(2,1)} %tokens_hbm.1, bf16[2048,1024]{1,0:T(8,128)(2,1)} %weight_hbm.1, bf16[192,2048]{1,0:T(8,128)(2,1)} %bitcast.2, bf16[192,256]{1,0:T(8,128)(2,1)} %bitcast.3, s32[12]{0:T(128)} %rank_hbm.1, s32[12]{0:T(128)} %slot_hbm.1, s32[1,32]{1,0:T(1,128)} %named_hbm.1, ...), custom_call_target="tpu_custom_call" | custom-call | tf_op jit(solution)/shard_map/pallas_call | solution.py:311
  45.4 1.7 %copy.10 = bf16[512,256]{1,0:T(8,128)(2,1)} copy(bf16[512,256]{1,0:T(8,128)(2,1)} %shard_map.82) | data formatting | bytes 524288
